TPU v7x, 32 devices: a whole 2x2x4 slice. The times are simulated.
32 devices in a mesh: group: 8 (over z, y), tp: 4 (over x, core).
Axes of the slice: x: 2, y: 2, z: 4, core: 2. Of those that a mesh axis runs over, the one named last changes fastest.
Arguments:
- pf_query: bfloat16 [2048, 8192], P('group', 'tp'), may hold values from -16 to 16
- pf_cache: bfloat16 [8, 2, 4096, 1024], P('group', None, 'tp'), may hold values from -16 to 16
- pf_offset: int32 [8], replicated, may hold values from 0 to 3840
- dec_query: bfloat16 [16, 8192], P('group', 'tp'), may hold values from -16 to 16
- dec_cache: bfloat16 [24, 2, 2048, 1024], P('group', None, 'tp'), may hold values from -16 to 16
- slot_owner: int32 [24], replicated, may hold values from 0 to 15, as said below
- slot_len: int32 [24], replicated, may hold values from 1 to 2048
Outputs:
- pf_out: bfloat16 [2048, 8192], P('group', 'tp')
- dec_out: bfloat16 [16, 8192], P('group', 'tp')
Inputs may be any that keep to these rules, and one draw needn't show every extreme that they name: `slot_owner`: every decode request owns one or two slots.
All inputs are finite; a program needn't handle non-finite values.
Results may differ from a plain program's by a relative error of at most 0.005.
Values may be sent and summed in bfloat16 or wider, within the bound.
A program may use at most 128 MiB of HBM per device.

v0:
```python
import jax
import jax.numpy as jnp
from jax import lax
from jax.sharding import PartitionSpec as P

QH = 64
KVH = 8
HD = 128


negative_big = -1e30


def merged_2(value, axis, join):
    pieces = jax.tree.map(lambda part: lax.all_gather(part, axis), value)
    head = jax.tree.map(lambda part: part[0], pieces)
    tail = jax.tree.map(lambda part: part[1:], pieces)
    running, _ = lax.scan(lambda running, share: (join(running, share), None), head, tail)
    return running


def attend_block(queries, cache_keys, cache_values, visible, score_scale):
    scores = (
        jnp.einsum("qgd,nd->gqn", queries, cache_keys, preferred_element_type=jnp.float32)
        * score_scale
    )
    scores = jnp.where(visible[None], scores, negative_big)
    maxima = jnp.max(scores, axis=-1)
    weights = jnp.where(visible[None], jnp.exp(scores - maxima[..., None]), 0.0).astype(
        jnp.bfloat16
    )
    totals = jnp.sum(weights, axis=-1, dtype=jnp.float32)
    weighted = jnp.einsum("gqn,nd->gqd", weights, cache_values, preferred_element_type=jnp.float32)
    return (maxima, totals, weighted)


def merge_along(maxima, totals, weighted, axis):
    largest = jnp.max(maxima, axis=axis, keepdims=True)
    factor = jnp.exp(maxima - largest)
    return (
        jnp.squeeze(largest, axis),
        jnp.sum(totals * factor, axis=axis),
        jnp.sum(weighted * factor[..., None], axis=axis),
    )


def combine_pair(first, second):
    largest = jnp.maximum(first[0], second[0])
    first_factor = jnp.exp(first[0] - largest)
    second_factor = jnp.exp(second[0] - largest)
    return (
        largest,
        first[1] * first_factor + second[1] * second_factor,
        first[2] * first_factor[..., None] + second[2] * second_factor[..., None],
    )


def masked_merge(hits, maxima, totals, weighted):
    selected_picks = jnp.where(hits[:, :, None], maxima[None], negative_big)
    largest = jnp.max(selected_picks, axis=1)
    factor = jnp.where(hits[:, :, None], jnp.exp(selected_picks - largest[:, None]), 0.0)
    denominator = jnp.einsum("abh,bh->ah", factor, totals, precision=lax.Precision.HIGHEST)
    numerator = jnp.einsum("abh,bhd->ahd", factor, weighted, precision=lax.Precision.HIGHEST)
    return (largest, denominator, numerator)


def on_device(pf_query, pf_cache, pf_offset, dec_query, dec_cache, slot_owner, slot_len):
    tp_count = lax.axis_size("tp")
    tp_rank = lax.axis_index("tp")
    group_rank = lax.axis_index("group")
    head_size = HD
    kv_heads = KVH
    width = QH // KVH
    local_heads = QH // tp_count
    score_scale = head_size ** (-0.5)
    pf_rows = pf_query.shape[0]
    local_len = pf_cache.shape[2]
    offset = lax.dynamic_index_in_dim(pf_offset, group_rank, keepdims=False)
    query_pos = offset + jnp.arange(pf_rows, dtype=jnp.int32)
    every_head = lax.all_gather(pf_query, "tp", axis=1, tiled=True)
    grouped = jnp.moveaxis(every_head.reshape(pf_rows, kv_heads, width, head_size), 1, 0)
    cache_keys = jnp.moveaxis(pf_cache[0, 0].reshape(local_len, kv_heads, head_size), 1, 0)
    cache_values = jnp.moveaxis(pf_cache[0, 1].reshape(local_len, kv_heads, head_size), 1, 0)
    key_pos = tp_rank * local_len + jnp.arange(local_len, dtype=jnp.int32)
    visible = key_pos[None, :] <= query_pos[:, None]
    maxima, totals, weighted = lax.map(
        lambda items: attend_block(items[0], items[1], items[2], visible, score_scale),
        (grouped, cache_keys, cache_values),
    )
    maxima = maxima.reshape(tp_count, local_heads, pf_rows)
    totals = totals.reshape(tp_count, local_heads, pf_rows)
    weighted = weighted.reshape(tp_count, local_heads, pf_rows, head_size)
    maxima, totals, weighted = (
        lax.all_to_all(maxima, "tp", split_axis=0, concat_axis=0, tiled=True),
        lax.all_to_all(totals, "tp", split_axis=0, concat_axis=0, tiled=True),
        lax.all_to_all(weighted, "tp", split_axis=0, concat_axis=0, tiled=True),
    )
    largest, denominator, numerator = merge_along(maxima, totals, weighted, 0)
    prefill_heads = numerator / denominator[..., None]
    pf_out = (
        jnp.moveaxis(prefill_heads, 1, 0)
        .reshape(pf_rows, local_heads * head_size)
        .astype(jnp.bfloat16)
    )
    served = dec_query.shape[0]
    head_queries_dec = lax.all_gather(dec_query, "tp", axis=1, tiled=True)
    all_queries = lax.all_gather(head_queries_dec, "group", axis=0, tiled=True)
    slots_here = dec_cache.shape[0]
    slot_local_len = dec_cache.shape[2]
    owners = lax.dynamic_slice_in_dim(slot_owner, group_rank * slots_here, slots_here)
    length_list = lax.dynamic_slice_in_dim(slot_len, group_rank * slots_here, slots_here)
    slot_queries = jnp.take(all_queries, owners, axis=0).reshape(
        slots_here, kv_heads, width, head_size
    )
    slot_keys = dec_cache[:, 0].reshape(slots_here, slot_local_len, kv_heads, head_size)
    slot_values = dec_cache[:, 1].reshape(slots_here, slot_local_len, kv_heads, head_size)
    scores = (
        jnp.einsum("skgd,slkd->skgl", slot_queries, slot_keys, preferred_element_type=jnp.float32)
        * score_scale
    )
    slot_pos = tp_rank * slot_local_len + jnp.arange(slot_local_len, dtype=jnp.int32)
    live = (slot_pos[None, :] < length_list[:, None])[:, None, None, :]
    scores = jnp.where(live, scores, negative_big)
    slot_max = jnp.max(scores, axis=-1)
    slot_weights = jnp.where(live, jnp.exp(scores - slot_max[..., None]), 0.0).astype(jnp.bfloat16)
    slot_totals = jnp.sum(slot_weights, axis=-1, dtype=jnp.float32)
    slot_weighted = jnp.einsum(
        "skgl,slkd->skgd", slot_weights, slot_values, preferred_element_type=jnp.float32
    )
    slot_max = slot_max.reshape(slots_here, QH)
    slot_totals = slot_totals.reshape(slots_here, QH)
    slot_weighted = slot_weighted.reshape(slots_here, QH, head_size)
    merged = merged_2((slot_max, slot_totals, slot_weighted), "tp", combine_pair)
    head_max = lax.dynamic_slice_in_dim(merged[0], tp_rank * local_heads, local_heads, 1)
    head_totals = lax.dynamic_slice_in_dim(merged[1], tp_rank * local_heads, local_heads, 1)
    head_weighted = lax.dynamic_slice_in_dim(merged[2], tp_rank * local_heads, local_heads, 1)
    every_max, every_totals, every_weighted = (
        lax.all_gather(head_max, "group", axis=0, tiled=True),
        lax.all_gather(head_totals, "group", axis=0, tiled=True),
        lax.all_gather(head_weighted, "group", axis=0, tiled=True),
    )
    mine = group_rank * served + jnp.arange(served, dtype=jnp.int32)
    hits = slot_owner[None, :] == mine[:, None]
    largest_dec, denominator_dec, numerator_dec = masked_merge(
        hits, every_max, every_totals, every_weighted
    )
    dec_out = (
        (numerator_dec / denominator_dec[..., None])
        .reshape(served, local_heads * head_size)
        .astype(jnp.bfloat16)
    )
    return (pf_out, dec_out)


def solution(mesh):
    placed = (
        P("group", "tp"),
        P("group", None, "tp", None),
        P(),
        P("group", "tp"),
        P("group", None, "tp", None),
        P(),
        P(),
    )
    return jax.shard_map(
        on_device,
        mesh=mesh,
        in_specs=placed,
        out_specs=(P("group", "tp"), P("group", "tp")),
        check_vma=False,
    )
```

profile of v0, /device:TPU:0, one launch (start us, length us, event | category | flops | bytes accessed | tf_op | source)
XLA Modules:
  0.0 403.5 jit_solution(4472428663473686276)
XLA Ops:
  9.5 4.0 fusion.46
  21.2 26.1 %all-gather.5.cloned.1.call-done = bf16[256,8192]{0,1:T(8,128)(2,1)} async-done(((bf16[256,2048]{0,1:T(8,128)(2,1)}), bf16[256,8192]{0,1:T(8,128)(2,1)}) %all-gather.5.cloned.1.call-update) | async-done | bytes 4194320 | tf_op jit(solution)/shard_map/all_gather | solution.py:80
  47.3 74.8 %while.30 = (s32[]{:T(128)}, f32[8,8,256]{2,1,0:T(8,128)S(1)}, f32[8,8,256]{2,1,0:T(8,128)S(1)}, f32[8,8,256,128]{3,2,1,0:T(8,128)}, bf16[8,1024,128]{1,2,0:T(8,...) while((s32[]{:T(128)}, f32[8,8,256]{2,1,0:T(8,128)S(1)}, ...), condition=%wide.region_3.4_spmd.clone, body=%wide.region_0.3_spmd.clone.sunk | while | flops 1105457152 | bytes 28384368 | solution.py:86
  52.2 4.6 %fusion.60 = f32[8,8,256,128]{3,2,1,0:T(8,128)} fusion(f32[8,8,256,128]{3,2,1,0:T(8,128)} %get-tuple-element.319, s32[]{:T(128)S(6)} %copy.81, bf16[8,1024,128]{1,2,0:T(8,128)(2,1)} %get-tuple-element.332, f32[1024,256,8]{1,0,2:T(8,128)S(1)} %get-tuple-element.303, f32[8,256]{1,0:T(8,128)S(1)} %get-tuple-element.302, ...), kind=kOutput, calls=%fused_computation.15.clone.1 | convolution fusion | flops 547356672 | bytes 9970688 | tf_op jit(solution)/shard_map/while/body/eval_jaxpr/gqn,nd->gqd/dot_general | solution.py:33
  61.6 4.5 %fusion.60 = f32[8,8,256,128]{3,2,1,0:T(8,128)} fusion(f32[8,8,256,128]{3,2,1,0:T(8,128)} %get-tuple-element.319, s32[]{:T(128)S(6)} %copy.81, bf16[8,1024,128]{1,2,0:T(8,128)(2,1)} %get-tuple-element.332, f32[1024,256,8]{1,0,2:T(8,128)S(1)} %get-tuple-element.303, f32[8,256]{1,0:T(8,128)S(1)} %get-tuple-element.302, ...), kind=kOutput, calls=%fused_computation.15.clone.1 | convolution fusion | flops 547356672 | bytes 9970688 | tf_op jit(solution)/shard_map/while/body/eval_jaxpr/gqn,nd->gqd/dot_general | solution.py:33
  70.9 4.5 %fusion.60 = f32[8,8,256,128]{3,2,1,0:T(8,128)} fusion(f32[8,8,256,128]{3,2,1,0:T(8,128)} %get-tuple-element.319, s32[]{:T(128)S(6)} %copy.81, bf16[8,1024,128]{1,2,0:T(8,128)(2,1)} %get-tuple-element.332, f32[1024,256,8]{1,0,2:T(8,128)S(1)} %get-tuple-element.303, f32[8,256]{1,0:T(8,128)S(1)} %get-tuple-element.302, ...), kind=kOutput, calls=%fused_computation.15.clone.1 | convolution fusion | flops 547356672 | bytes 9970688 | tf_op jit(solution)/shard_map/while/body/eval_jaxpr/gqn,nd->gqd/dot_general | solution.py:33
  80.3 4.5 %fusion.60 = f32[8,8,256,128]{3,2,1,0:T(8,128)} fusion(f32[8,8,256,128]{3,2,1,0:T(8,128)} %get-tuple-element.319, s32[]{:T(128)S(6)} %copy.81, bf16[8,1024,128]{1,2,0:T(8,128)(2,1)} %get-tuple-element.332, f32[1024,256,8]{1,0,2:T(8,128)S(1)} %get-tuple-element.303, f32[8,256]{1,0:T(8,128)S(1)} %get-tuple-element.302, ...), kind=kOutput, calls=%fused_computation.15.clone.1 | convolution fusion | flops 547356672 | bytes 9970688 | tf_op jit(solution)/shard_map/while/body/eval_jaxpr/gqn,nd->gqd/dot_general | solution.py:33
  89.6 4.5 %fusion.60 = f32[8,8,256,128]{3,2,1,0:T(8,128)} fusion(f32[8,8,256,128]{3,2,1,0:T(8,128)} %get-tuple-element.319, s32[]{:T(128)S(6)} %copy.81, bf16[8,1024,128]{1,2,0:T(8,128)(2,1)} %get-tuple-element.332, f32[1024,256,8]{1,0,2:T(8,128)S(1)} %get-tuple-element.303, f32[8,256]{1,0:T(8,128)S(1)} %get-tuple-element.302, ...), kind=kOutput, calls=%fused_computation.15.clone.1 | convolution fusion | flops 547356672 | bytes 9970688 | tf_op jit(solution)/shard_map/while/body/eval_jaxpr/gqn,nd->gqd/dot_general | solution.py:33
  99.0 4.5 %fusion.60 = f32[8,8,256,128]{3,2,1,0:T(8,128)} fusion(f32[8,8,256,128]{3,2,1,0:T(8,128)} %get-tuple-element.319, s32[]{:T(128)S(6)} %copy.81, bf16[8,1024,128]{1,2,0:T(8,128)(2,1)} %get-tuple-element.332, f32[1024,256,8]{1,0,2:T(8,128)S(1)} %get-tuple-element.303, f32[8,256]{1,0:T(8,128)S(1)} %get-tuple-element.302, ...), kind=kOutput, calls=%fused_computation.15.clone.1 | convolution fusion | flops 547356672 | bytes 9970688 | tf_op jit(solution)/shard_map/while/body/eval_jaxpr/gqn,nd->gqd/dot_general | solution.py:33
  108.3 4.5 %fusion.60 = f32[8,8,256,128]{3,2,1,0:T(8,128)} fusion(f32[8,8,256,128]{3,2,1,0:T(8,128)} %get-tuple-element.319, s32[]{:T(128)S(6)} %copy.81, bf16[8,1024,128]{1,2,0:T(8,128)(2,1)} %get-tuple-element.332, f32[1024,256,8]{1,0,2:T(8,128)S(1)} %get-tuple-element.303, f32[8,256]{1,0:T(8,128)S(1)} %get-tuple-element.302, ...), kind=kOutput, calls=%fused_computation.15.clone.1 | convolution fusion | flops 547356672 | bytes 9970688 | tf_op jit(solution)/shard_map/while/body/eval_jaxpr/gqn,nd->gqd/dot_general | solution.py:33
  117.6 4.5 %fusion.60 = f32[8,8,256,128]{3,2,1,0:T(8,128)} fusion(f32[8,8,256,128]{3,2,1,0:T(8,128)} %get-tuple-element.319, s32[]{:T(128)S(6)} %copy.81, bf16[8,1024,128]{1,2,0:T(8,128)(2,1)} %get-tuple-element.332, f32[1024,256,8]{1,0,2:T(8,128)S(1)} %get-tuple-element.303, f32[8,256]{1,0:T(8,128)S(1)} %get-tuple-element.302, ...), kind=kOutput, calls=%fused_computation.15.clone.1 | convolution fusion | flops 547356672 | bytes 9970688 | tf_op jit(solution)/shard_map/while/body/eval_jaxpr/gqn,nd->gqd/dot_general | solution.py:33
  122.1 7.1 %all_to_all.15 = f32[4,16,256]{2,1,0:T(8,128)} all-to-all(f32[4,16,256]{2,1,0:T(8,128)S(1)} %bitcast.139), channel_id=1, replica_groups=mesh['group'=8,'tp'=4] {'tp'}, dimensions={0} | all-to-all | bytes 131072 | tf_op jit(solution)/shard_map/all_to_all | solution.py:95
  129.2 7.1 %all_to_all.16 = f32[4,16,256]{2,1,0:T(8,128)} all-to-all(f32[4,16,256]{2,1,0:T(8,128)S(1)} %bitcast.138), channel_id=1, replica_groups=mesh['group'=8,'tp'=4] {'tp'}, dimensions={0} | all-to-all | bytes 131072 | tf_op jit(solution)/shard_map/all_to_all | solution.py:94
  136.4 5.7 %all-to-all-start = ((f32[4,16,256,128]{3,2,1,0:T(8,128)}), f32[4,16,256,128]{3,2,1,0:T(8,128)}, u32[]{:S(2)}, u32[]{:S(2)}) async-start(f32[4,16,256,128]{3,2,1,0:T(8,128)} %bitcast.130), calls=%async_computation | async-start | bytes 16777216 | tf_op jit(solution)/shard_map/all_to_all | solution.py:96
  142.1 6.9 %fusion.45 = (bf16[3,1,512,1024]{3,2,1,0:T(8,128)(2,1)}, bf16[3,1,512,1024]{3,2,1,0:T(8,128)(2,1)}) fusion(bf16[3,2,512,1024]{3,2,1,0:T(8,128)(2,1)} %param.15), kind=kLoop, calls=%fused_computation.81 | loop fusion | bytes 12582912 | tf_op jit(solution)/shard_map/slice | solution.py:116
  152.2 84.0 %all_gather.28 = bf16[2,8192]{1,0:T(2,128)(2,1)S(1)} all-gather(bf16[2,2048]{1,0:T(2,128)(2,1)S(1)} %copy-done.2), channel_id=1, replica_groups=mesh['group'=8,'tp'=4] {'tp'}, dimensions={1}, use_global_device_ids=true | all-gather | bytes 40960 | tf_op jit(solution)/shard_map/all_gather | solution.py:106
  236.2 32.8 %all-gather = bf16[8,2,8192]{2,1,0:T(2,128)(2,1)} all-gather(bf16[1,2,8192]{2,1,0:T(2,128)(2,1)S(1)} %bitcast.136), channel_id=1, replica_groups=mesh['group'=8,'tp'=4] {'group'}, dimensions={0}, use_global_device_ids=true | all-gather | bytes 294912 | tf_op jit(solution)/shard_map/all_gather | solution.py:107
  278.3 5.3 %all_gather.30 = f32[4,3,64]{2,1,0:T(4,128)S(1)} all-gather(f32[1,3,64]{2,1,0:T(4,128)} %all_gather_reshape.9), channel_id=1, replica_groups=mesh['group'=8,'tp'=4] {'tp'}, dimensions={0}, use_global_device_ids=true | all-gather | bytes 3840 | tf_op jit(solution)/shard_map/all_gather | solution.py:15
  284.2 5.3 %all_gather.31 = f32[4,3,64]{2,1,0:T(4,128)S(1)} all-gather(f32[1,3,64]{2,1,0:T(4,128)} %all_gather_reshape.10), channel_id=1, replica_groups=mesh['group'=8,'tp'=4] {'tp'}, dimensions={0}, use_global_device_ids=true | all-gather | bytes 3840 | tf_op jit(solution)/shard_map/all_gather | solution.py:15
  291.0 6.5 %all_gather.32 = f32[4,3,64,128]{3,2,1,0:T(8,128)S(1)} all-gather(f32[1,3,64,128]{3,2,1,0:T(8,128)S(1)} %convolution_bitcast_fusion.1), channel_id=1, replica_groups=mesh['group'=8,'tp'=4] {'tp'}, dimensions={0}, use_global_device_ids=true | all-gather | bytes 491520 | tf_op jit(solution)/shard_map/all_gather | solution.py:15
  301.6 26.0 %all-gather.2 = f32[8,3,16]{2,1,0:T(4,128)S(1)} all-gather(f32[1,3,16]{2,1,0:T(4,128)S(1)} %dynamic-slice_bitcast_fusion), channel_id=1, replica_groups=mesh['group'=8,'tp'=4] {'group'}, dimensions={0}, use_global_device_ids=true | all-gather | bytes 1728 | tf_op jit(solution)/shard_map/all_gather | solution.py:139
  327.8 26.2 %all-gather.1 = f32[8,3,16]{2,1,0:T(4,128)S(1)} all-gather(f32[1,3,16]{2,1,0:T(4,128)S(1)} %dynamic-slice_bitcast_fusion.1), channel_id=1, replica_groups=mesh['group'=8,'tp'=4] {'group'}, dimensions={0}, use_global_device_ids=true | all-gather | bytes 1728 | tf_op jit(solution)/shard_map/all_gather | solution.py:138
  354.0 30.6 %all_gather.33 = f32[24,16,128]{2,1,0:T(8,128)S(1)} all-gather(f32[3,16,128]{2,1,0:T(8,128)S(1)} %constant_dynamic-slice_fusion), channel_id=1, replica_groups=mesh['group'=8,'tp'=4] {'group'}, dimensions={0}, use_global_device_ids=true | all-gather | bytes 221184 | tf_op jit(solution)/shard_map/all_gather | solution.py:140
  388.5 5.4 %multiply_reduce_fusion = f32[16,256,128]{2,1,0:T(8,128)S(1)} fusion(f32[4,16,256,128]{3,2,1,0:T(8,128)} %all-to-all-done, f32[4,16,256]{2,1,0:T(8,128)S(1)} %get-tuple-element.181), kind=kLoop, calls=%fused_computation.28 | loop fusion | flops 3670016 | bytes 10551296 | tf_op jit(solution)/shard_map/reduce_sum | solution.py:43
  (100 shorter events, 76.6 us)
Async XLA Ops:
  7.2 40.2 %all-gather.5.cloned.1.call-start = ((), (), s32[]{:S(2)}) async-start(), calls=%async_computation.3 | async-start | bytes 5242880 | tf_op jit(solution)/shard_map/all_gather | solution.py:80
  13.5 6.5 %copy-start.4 = (s32[8]{0:T(128)S(1)}, s32[8]{0:T(128)}, u32[]{:S(2)}) copy-start(s32[8]{0:T(128)} %param.13) | copy-start | bytes 100
  136.4 252.1 %all-to-all-start = ((f32[4,16,256,128]{3,2,1,0:T(8,128)}), f32[4,16,256,128]{3,2,1,0:T(8,128)}, u32[]{:S(2)}, u32[]{:S(2)}) async-start(f32[4,16,256,128]{3,2,1,0:T(8,128)} %bitcast.130), calls=%async_computation | async-start | bytes 16777216 | tf_op jit(solution)/shard_map/all_to_all | solution.py:96
  149.0 3.2 copy-start.2
  149.0 121.1 %copy-start.5 = (s32[24]{0:T(128)S(1)}, s32[24]{0:T(128)}, u32[]{:S(2)}) copy-start(s32[24]{0:T(128)} %param.17) | copy-start | bytes 292
  149.0 121.2 %copy-start.3 = (s32[24]{0:T(128)S(1)}, s32[24]{0:T(128)}, u32[]{:S(2)}) copy-start(s32[24]{0:T(128)} %param.16) | copy-start | bytes 292
  283.6 6.5 %copy-start = (f32[4,3,64]{2,1,0:T(4,128)}, f32[4,3,64]{2,1,0:T(4,128)S(1)}, u32[]{:S(2)}) copy-start(f32[4,3,64]{2,1,0:T(4,128)S(1)} %all_gather.30) | copy-start | bytes 9220
  289.4 0.6 copy-start.1
Sparse Core Ops, SparseCore 0:
  10.1 37.1 all-gather.4
where the time goes:
time: 405 us; the launch traced here: 403 us
  blocking collectives  231 us (57%)
  matrix products  60.3 us (15%)
  local copies, waits for them, and re-layouts  35.3 us (9%)
  other arithmetic  30.4 us (8%)
  waiting for transfers between devices  26.1 us (6%)
  between operations  14.2 us (4%)
  starting transfers between devices  5.69 us (1%)
    all_gather x1, blocking collectives, on_device(): head_queries_dec = lax.all_gather(dec_query, 'tp', axis=1, tiled=True)  84 us
    dot_general x8, matrix products, attend_block(): jnp.einsum('gqn,nd->gqd', weights, cache_values, preferred_element_type=j...  35.9 us
    all_gather x1, blocking collectives, on_device(): all_queries = lax.all_gather(head_queries_dec, 'group', axis=0, tiled=True)  32.8 us
    all_gather x1, blocking collectives, on_device(): lax.all_gather(head_weighted, 'group', axis=0, tiled=True)  30.6 us
    all_gather x1, blocking collectives, on_device(): lax.all_gather(head_max, 'group', axis=0, tiled=True)  26.2 us
    all_gather x1, waiting for transfers between devices, on_device(): every_head = lax.all_gather(pf_query, 'tp', axis=1, tiled=True)  26.1 us
    all_gather x1, blocking collectives, on_device(): lax.all_gather(head_totals, 'group', axis=0, tiled=True)  26 us
    dot_general x8, matrix products, attend_block(): jnp.einsum('qgd,nd->gqn', queries, cache_keys, preferred_element_type=jnp...  20.8 us
  transfers between devices with their start and end apart: 2, of which 1 were waited for; matrix products, arithmetic and copies ran while one was open for 10% of the time, Pallas kernels for 0%

commit v1 on v0

v1 whole, which is shorter than its diff:
```python
import functools
import math
import jax
import jax.numpy as jnp
from jax import lax
from jax.experimental import pallas as pl
from jax.experimental.pallas import tpu as pltpu
from jax.sharding import PartitionSpec as P

QH = 64
KVH = 8
HD = 128
WIDTH = QH // KVH
LOW = -1e30
SCALE = HD ** (-0.5) * math.log2(math.e)
DIMS_NT = (((1,), (1,)), ((), ()))


def kernel(cfg, off_ref, own_ref, len_ref, q_hbm, kv_hbm, dq_hbm, dkv_hbm, out_ref, dout_ref,
           q_ref, kvbuf, dkv, bias, acc, mrow, dqbuf, dpart, dpeer, dall,
           loc_sem, own_sem, kv_send, kv_recv, dq1_send, dq1_recv, dq2_send, dq2_recv,
           dp_send, dp_recv, da_send, da_recv):
    tp, groups, rows, llen, block, lh, kvl, served, slots, slen = cfg
    pieces = llen // block
    chips = tp // 2
    cols = kvl * HD
    t = lax.axis_index("tp")
    g = lax.axis_index("group")
    chip, core = t // 2, t % 2

    def source(s):
        return lax.rem(chip + s // 2, chips) * 2 + lax.rem(core + s % 2, 2)

    def target(s):
        return lax.rem(chip + chips - s // 2, chips) * 2 + lax.rem(core + s % 2, 2)

    def kv_copy(s, piece):
        dest = target(s)
        col = pl.multiple_of((dest * lh // WIDTH) * HD, HD)
        at = pl.ds(piece * block, block)
        return pltpu.make_async_remote_copy(
            src_ref=kv_hbm.at[0, :, at, pl.ds(col, cols)],
            dst_ref=kvbuf.at[s, :, at, :],
            send_sem=kv_send.at[s, piece],
            recv_sem=kv_recv.at[s, piece],
            device_id={"tp": dest},
            device_id_type=pl.DeviceIdType.MESH,
        )

    def own_copy(piece):
        col = pl.multiple_of((t * lh // WIDTH) * HD, HD)
        at = pl.ds(piece * block, block)
        return pltpu.make_async_copy(
            kv_hbm.at[0, :, at, pl.ds(col, cols)], kvbuf.at[0, :, at, :], own_sem.at[piece])

    def dq1_copy(i):
        return pltpu.make_async_remote_copy(
            src_ref=dq_hbm, dst_ref=dqbuf.at[g, :, t], send_sem=dq1_send.at[i],
            recv_sem=dq1_recv.at[i], device_id={"tp": lax.rem(t + i, tp)},
            device_id_type=pl.DeviceIdType.MESH)

    def dq2_copy(i):
        return pltpu.make_async_remote_copy(
            src_ref=dqbuf.at[g], dst_ref=dqbuf.at[g], send_sem=dq2_send.at[i],
            recv_sem=dq2_recv.at[i], device_id={"group": lax.rem(g + i, groups)},
            device_id_type=pl.DeviceIdType.MESH)

    def dp_copy(i):
        dest = lax.rem(t + i, tp)
        return pltpu.make_async_remote_copy(
            src_ref=dpart.at[dest], dst_ref=dpeer.at[i], send_sem=dp_send.at[i],
            recv_sem=dp_recv.at[i], device_id={"tp": dest},
            device_id_type=pl.DeviceIdType.MESH)

    def da_copy(i):
        return pltpu.make_async_remote_copy(
            src_ref=dall.at[g], dst_ref=dall.at[g], send_sem=da_send.at[i],
            recv_sem=da_recv.at[i], device_id={"group": lax.rem(g + i, groups)},
            device_id_type=pl.DeviceIdType.MESH)

    q_copy = pltpu.make_async_copy(q_hbm, q_ref, loc_sem.at[0])
    dq0_copy = pltpu.make_async_copy(dq_hbm, dqbuf.at[g, :, t], loc_sem.at[1])
    dkv_copy = pltpu.make_async_copy(dkv_hbm, dkv, loc_sem.at[2])
    q_copy.start()
    for p in range(pieces):
        own_copy(p).start()
    dq0_copy.start()

    barrier = pltpu.get_barrier_semaphore()
    for i in range(1, tp):
        pl.semaphore_signal(barrier, inc=1, device_id={"tp": lax.rem(t + i, tp)},
                            device_id_type=pl.DeviceIdType.MESH)
    for i in range(1, groups):
        pl.semaphore_signal(barrier, inc=1, device_id={"group": lax.rem(g + i, groups)},
                            device_id_type=pl.DeviceIdType.MESH)
    acc[...] = jnp.zeros_like(acc)
    mrow[...] = jnp.full_like(mrow, LOW)
    pl.semaphore_wait(barrier, tp - 1 + groups - 1)

    for i in range(1, tp):
        dq1_copy(i).start()
    for j in range(1, chips):
        for p in range(pieces):
            for i in range(2):
                kv_copy(2 * j + i, p).start()
    for p in range(pieces):
        kv_copy(1, p).start()
    dkv_copy.start()

    offset = off_ref[g]

    def attend(s, piece):
        at = pl.ds(piece * block, block)
        base = source(s) * llen + piece * block
        pos = lax.broadcasted_iota(jnp.int32, (rows, block), 1) + base
        tok = lax.broadcasted_iota(jnp.int32, (rows, block), 0) + offset
        bias[...] = jnp.where(pos <= tok, 0.0, LOW)

        def one(h):
            kcol = pl.ds(pl.multiple_of((h // WIDTH) * HD, HD), HD)
            q = q_ref[:, pl.ds(pl.multiple_of(h * HD, HD), HD)]
            k = kvbuf[s, 0, at, kcol]
            v = kvbuf[s, 1, at, kcol]
            sc = lax.dot_general(q, k, DIMS_NT, preferred_element_type=jnp.float32)
            sc = sc * SCALE + bias[...]
            old = mrow[h]
            new = jnp.maximum(old, jnp.max(sc, axis=1, keepdims=True))
            w = jnp.exp2(sc - new[:, :1]).astype(jnp.bfloat16)
            vx = jnp.concatenate([v, jnp.ones_like(v)], axis=1)
            o = jnp.dot(w, vx, preferred_element_type=jnp.float32)
            factor = jnp.exp2(old - new)
            mrow[h] = new
            acc[h] = acc[h] * jnp.concatenate([factor, factor], axis=1) + o

        def pair(b, carry):
            one(2 * b)
            one(2 * b + 1)
            return carry

        lax.fori_loop(0, lh // 2, pair, 0)

    def own_step(p, carry):
        own_copy(p).wait()
        attend(0, p)
        return carry

    def near_step(p, carry):
        kv_copy(1, p).wait_recv()
        attend(1, p)
        return carry

    def far_step(b, carry):
        j = 1 + b // (2 * pieces)
        c = b % (2 * pieces)
        s, p = 2 * j + c % 2, c // 2
        kv_copy(s, p).wait_recv()
        attend(s, p)
        return carry

    q_copy.wait()
    lax.fori_loop(0, pieces, own_step, 0)

    dq0_copy.wait()
    for i in range(1, tp):
        dq1_copy(i).wait_recv()
    for i in range(1, groups):
        dq2_copy(i).start()

    lax.fori_loop(0, pieces, near_step, 0)

    dkv_copy.wait()
    for i in range(1, groups):
        dq2_copy(i).wait_recv()
    for n in range(slots):
        owner = own_ref[g * slots + n]
        query = dqbuf[owner // served, owner % served].reshape(QH, HD)
        wide = jnp.concatenate([query] * KVH, axis=1)
        r = lax.broadcasted_iota(jnp.int32, (QH, KVH * HD), 0) // WIDTH
        c = lax.broadcasted_iota(jnp.int32, (QH, KVH * HD), 1) // HD
        wide = jnp.where(r == c, wide, 0.0).astype(jnp.bfloat16)
        sc = lax.dot_general(wide, dkv[n, 0], DIMS_NT, preferred_element_type=jnp.float32)
        pos = lax.broadcasted_iota(jnp.int32, (QH, slen), 1) + t * slen
        live = pos < len_ref[g * slots + n]
        sc = jnp.where(live, sc * SCALE, LOW)
        top = jnp.max(sc, axis=1, keepdims=True)
        w = jnp.where(live, jnp.exp2(sc - top), 0.0).astype(jnp.bfloat16)
        total = jnp.sum(w.astype(jnp.float32), axis=1, keepdims=True)
        o = jnp.dot(w, dkv[n, 1], preferred_element_type=jnp.float32)
        o = jnp.concatenate(
            [o[k * WIDTH:(k + 1) * WIDTH, k * HD:(k + 1) * HD] for k in range(KVH)], axis=0)
        lane = lax.broadcasted_iota(jnp.int32, (QH, HD), 1)
        stat = jnp.where(lane < HD // 2, top, total)
        for d in range(tp):
            dpart[d, 0, n] = o[d * lh:(d + 1) * lh]
            dpart[d, 1, n] = stat[d * lh:(d + 1) * lh]
    for i in range(1, tp):
        dp_copy(i).start()

    far = 2 * (chips - 1) * pieces
    cut = far // 2
    lax.fori_loop(0, cut, far_step, 0)

    for i in range(1, tp):
        dp_copy(i).wait_recv()
    half = HD // 2
    for n in range(slots):
        accs = [dpart[t, 0, n]] + [dpeer[i, 0, n] for i in range(1, tp)]
        stats = [dpart[t, 1, n]] + [dpeer[i, 1, n] for i in range(1, tp)]
        top = functools.reduce(jnp.maximum, [x[:, :1] for x in stats])
        fac = [jnp.exp2(x[:, :1] - top) for x in stats]
        total = sum(f * x[:, half:half + 1] for f, x in zip(fac, stats))
        lane = lax.broadcasted_iota(jnp.int32, (lh, HD), 1)
        dall[g, 0, n] = sum(f * a for f, a in zip(fac, accs))
        dall[g, 1, n] = jnp.where(lane < half, top, total)
    for i in range(1, groups):
        da_copy(i).start()

    lax.fori_loop(cut, far, far_step, 0)

    def finish(h, carry):
        a = acc[h]
        out_ref[:, pl.ds(pl.multiple_of(h * HD, HD), HD)] = (
            a[:, :HD] / a[:, HD:]).astype(out_ref.dtype)
        return carry

    lax.fori_loop(0, lh, finish, 0)

    for i in range(1, groups):
        da_copy(i).wait_recv()
    for r in range(served):
        mine = g * served + r

        def peak(e, top):
            for n in range(slots):
                m = jnp.broadcast_to(dall[e, 1, n][:, :1], (lh, HD))
                top = jnp.maximum(top, jnp.where(own_ref[e * slots + n] == mine, m, LOW))
            return top

        top = lax.fori_loop(0, groups, peak, jnp.full((lh, HD), LOW, jnp.float32))

        def gather(e, carry):
            num, den = carry
            for n in range(slots):
                x = dall[e, 1, n]
                hit = own_ref[e * slots + n] == mine
                f = jnp.where(hit, jnp.exp2(jnp.minimum(x[:, :1] - top, 0.0)), 0.0)
                num = num + f * dall[e, 0, n]
                den = den + f * x[:, half:half + 1]
            return num, den

        zero = jnp.zeros((lh, HD), jnp.float32)
        num, den = lax.fori_loop(0, groups, gather, (zero, zero))
        dout_ref[r] = (num / den).astype(dout_ref.dtype)

    for i in range(1, tp):
        dq1_copy(i).wait_send()
        dp_copy(i).wait_send()
    for i in range(1, groups):
        dq2_copy(i).wait_send()
        da_copy(i).wait_send()
    for s in range(1, tp):
        for p in range(pieces):
            kv_copy(s, p).wait_send()


def on_device(pf_query, pf_cache, pf_offset, dec_query, dec_cache, slot_owner, slot_len):
    tp = lax.axis_size("tp")
    groups = lax.axis_size("group")
    rows, llen = pf_query.shape[0], pf_cache.shape[2]
    lh = QH // tp
    kvl = max(1, lh // WIDTH)
    served, slots, slen = dec_query.shape[0], dec_cache.shape[0], dec_cache.shape[2]
    block = min(512, llen)
    pieces = llen // block
    cfg = (tp, groups, rows, llen, block, lh, kvl, served, slots, slen)
    dq = dec_query.reshape(served, lh, HD).astype(jnp.float32)
    dma = pltpu.SemaphoreType.DMA
    smem = pl.BlockSpec(memory_space=pltpu.SMEM)
    anywhere = pl.BlockSpec(memory_space=pl.ANY)
    vmem = pl.BlockSpec(memory_space=pltpu.VMEM)
    pf_out, dec_out = pl.pallas_call(
        functools.partial(kernel, cfg),
        out_shape=(
            jax.ShapeDtypeStruct((rows, lh * HD), jnp.bfloat16),
            jax.ShapeDtypeStruct((served, lh, HD), jnp.bfloat16),
        ),
        in_specs=[smem, smem, smem, anywhere, anywhere, anywhere, anywhere],
        out_specs=(vmem, vmem),
        scratch_shapes=[
            pltpu.VMEM((rows, lh * HD), jnp.bfloat16),
            pltpu.VMEM((tp, 2, llen, kvl * HD), jnp.bfloat16),
            pltpu.VMEM(dec_cache.shape, jnp.bfloat16),
            pltpu.VMEM((rows, block), jnp.float32),
            pltpu.VMEM((lh, rows, 2 * HD), jnp.float32),
            pltpu.VMEM((lh, rows, HD), jnp.float32),
            pltpu.VMEM((groups, served, tp, lh, HD), jnp.float32),
            pltpu.VMEM((tp, 2, slots, lh, HD), jnp.float32),
            pltpu.VMEM((tp, 2, slots, lh, HD), jnp.float32),
            pltpu.VMEM((groups, 2, slots, lh, HD), jnp.float32),
            dma((3,)),
            dma((pieces,)),
            dma((tp, pieces)),
            dma((tp, pieces)),
            dma((tp,)),
            dma((tp,)),
            dma((groups,)),
            dma((groups,)),
            dma((tp,)),
            dma((tp,)),
            dma((groups,)),
            dma((groups,)),
        ],
        compiler_params=pltpu.CompilerParams(
            collective_id=0, has_side_effects=True, vmem_limit_bytes=48 * 1024 * 1024),
    )(pf_offset, slot_owner, slot_len, pf_query, pf_cache, dq, dec_cache)
    return pf_out, dec_out.reshape(served, lh * HD)


def solution(mesh):
    placed = (
        P("group", "tp"),
        P("group", None, "tp", None),
        P(),
        P("group", "tp"),
        P("group", None, "tp", None),
        P(),
        P(),
    )
    return jax.shard_map(
        on_device,
        mesh=mesh,
        in_specs=placed,
        out_specs=(P("group", "tp"), P("group", "tp")),
        check_vma=False,
    )
```

time: 405 us -> 81.1 us (0.20)
  blocking collectives: 231 us -> 0 us
  Pallas kernels: 0 us -> 74.8 us
  matrix products: 60.3 us -> 0 us
  local copies, waits for them, and re-layouts: 35.3 us -> 4.76 us
  other arithmetic: 30.4 us -> 0.7 us
  waiting for transfers between devices: 26.1 us -> 0 us
  between operations: 14.2 us -> 0.65 us
  starting transfers between devices: 5.69 us -> 0 us
    all_gather x8 -> x0, blocking collectives: 217 us -> none  [the longest x1 84 us: on_device(): head_queries_dec = lax.all_gather(dec_query, 'tp', axis=1, tiled=True)]
    pallas_call x0 -> x1, Pallas kernels: none -> 74.8 us  [on_device(): pl.pallas_call(functools.partial(kernel, cfg), out_shape=(jax.ShapeDtypeS...]
    dot_general x20 -> x0, matrix products: 60.3 us -> none  [the longest x8 35.9 us: attend_block(): jnp.einsum('gqn,nd->gqd', weights, cache_values, preferred_element_type=j...]
    all_gather x1 -> x0, waiting for transfers between devices: 26.1 us -> none  [on_device(): every_head = lax.all_gather(pf_query, 'tp', axis=1, tiled=True)]
    reduce_sum x11 -> x0, other arithmetic: 22.6 us -> none  [the longest x8 16.1 us: attend_block(): totals = jnp.sum(weights, axis=-1, dtype=jnp.float32)]
    all_to_all x2 -> x0, blocking collectives: 14.3 us -> none  [the longest x1 7.15 us: on_device(): lax.all_to_all(maxima, 'tp', split_axis=0, concat_axis=0, tiled=True)]
    unnamed x25 -> x11, local copies, waits for them, and re-layouts: 18 us -> 4.76 us
    slice x5 -> x0, local copies, waits for them, and re-layouts: 12.1 us -> none  [the longest x1 6.9 us: on_device(): dec_cache[:, 1].reshape(slots_here, slot_local_len, kv_heads, head_size)]
  transfers between devices with their start and end apart: 2 -> 0, of which waited for: 1 -> 0; matrix products, arithmetic and copies ran while one was open for 10% -> 0% of each run, Pallas kernels for 0% -> 0%
where the time goes in v1:
time: 81.1 us; the launch traced here: 80.9 us
  Pallas kernels  74.8 us (92%)
  local copies, waits for them, and re-layouts  4.76 us (6%)
    pallas_call x1, Pallas kernels, on_device(): pl.pallas_call(functools.partial(kernel, cfg), out_shape=(jax.ShapeDtypeS...  74.8 us
    unnamed x11, local copies, waits for them, and re-layouts  4.76 us

profile of v1, /device:TPU:0, one launch (start us, length us, event | category | flops | bytes accessed | tf_op | source)
XLA Modules:
  0.0 80.9 jit_solution(9969909686673993883)
XLA Ops:
  0.6 0.7 convert_bitcast_fusion
  1.3 0.0 copy-start
  1.4 1.2 %copy-done = bf16[256,2048]{1,0:T(8,128)(2,1)S(1)} copy-done((bf16[256,2048]{1,0:T(8,128)(2,1)S(1)}, bf16[256,2048]{1,0:T(8,128)(2,1)}, u32[]{:S(2)}) %copy-start) | copy-done | bytes 1048600
  2.6 0.0 copy-start.1
  2.6 0.7 copy-done.1
  3.2 0.0 copy-start.2
  3.2 0.7 copy-done.2
  3.9 0.0 copy-start.3
  3.9 0.7 copy-done.3
  4.5 74.8 %shard_map.86 = (bf16[256,2048]{1,0:T(8,128)(2,1)S(1)}, bf16[2,16,128]{2,1,0:T(8,128)(2,1)S(1)}) custom-call(s32[8]{0:T(128)S(1)} %copy-done.1, s32[24]{0:T(128)S(1)} %copy-done.2, s32[24]{0:T(128)S(1)} %copy-done.3, bf16[256,2048]{1,0:T(8,128)(2,1)S(1)} %copy-done, bf16[1,2,1024,1024]{3,2,1,0:T(8,128)(2,1)} %kv_hbm.1, f32[2,16,128]{2,1,0:T(8,128)S(1)} %bitcast.9, ...), custom_call_target="tpu_custom_call" | custom-call | tf_op jit(solution)/shard_map/pallas_call | solution.py:281
  79.3 0.6 copy.14
  79.9 1.0 %copy.16 = bf16[256,2048]{1,0:T(8,128)(2,1)} copy(bf16[256,2048]{1,0:T(8,128)(2,1)S(1)} %get-tuple-element.8) | data formatting | bytes 2097152
  (1 shorter events, 0.0 us)
Async XLA Ops:
  1.3 1.2 %copy-start = (bf16[256,2048]{1,0:T(8,128)(2,1)S(1)}, bf16[256,2048]{1,0:T(8,128)(2,1)}, u32[]{:S(2)}) copy-start(bf16[256,2048]{1,0:T(8,128)(2,1)} %q_hbm.1) | copy-start | bytes 3145732
  2.6 0.7 copy-start.1
  3.2 0.7 copy-start.2
  3.9 0.7 copy-start.3

commit v2 on v1

v2 whole, which is shorter than its diff:
```python
import functools
import math
import jax
import jax.numpy as jnp
from jax import lax
from jax.experimental import pallas as pl
from jax.experimental.pallas import tpu as pltpu
from jax.sharding import PartitionSpec as P

QH = 64
KVH = 8
HD = 128
WIDTH = QH // KVH
LOW = -1e30
STACK = 2
EXTRA = 16
SCALE = HD ** (-0.5) * math.log2(math.e)


def kernel(cfg, off_hbm, own_hbm, len_hbm, q_hbm, kv_hbm, dq_hbm, dkv_hbm, out_ref, dout_ref,
           off_ref, own_ref, len_ref, q_ref, dq_ref, q2, kvbuf, dkv, vt, bias, acc, mrow, dqtp, dqbuf,
           dpart, dpeer, dall, loc_sem, own_sem, kv_send, kv_recv, dq1_send, dq1_recv, dq2_send, dq2_recv,
           dp_send, dp_recv, da_send, da_recv):
    tp, groups, rows, llen, block, stack, lh, kvl, served, slots, slen = cfg
    pieces = llen // block
    chips = tp // 2
    cols = kvl * HD
    t = lax.axis_index("tp")
    g = lax.axis_index("group")
    chip, core = t // 2, t % 2

    def source(s):
        return lax.rem(chip + s // 2, chips) * 2 + lax.rem(core + s % 2, 2)

    def target(s):
        return lax.rem(chip + chips - s // 2, chips) * 2 + lax.rem(core + s % 2, 2)

    def kv_copy(s, piece):
        dest = target(s)
        col = pl.multiple_of((dest * lh // WIDTH) * HD, HD)
        at = pl.ds(piece * block, block)
        return pltpu.make_async_remote_copy(
            src_ref=kv_hbm.at[0, :, at, pl.ds(col, cols)],
            dst_ref=kvbuf.at[s, :, at, :],
            send_sem=kv_send.at[s, piece],
            recv_sem=kv_recv.at[s, piece],
            device_id={"tp": dest},
            device_id_type=pl.DeviceIdType.MESH,
        )

    def own_copy(piece):
        col = pl.multiple_of((t * lh // WIDTH) * HD, HD)
        at = pl.ds(piece * block, block)
        return pltpu.make_async_copy(
            kv_hbm.at[0, :, at, pl.ds(col, cols)], kvbuf.at[0, :, at, :], own_sem.at[piece])

    def dq1_copy(i):
        return pltpu.make_async_remote_copy(
            src_ref=dqtp.at[t], dst_ref=dqtp.at[t], send_sem=dq1_send.at[i],
            recv_sem=dq1_recv.at[i], device_id={"tp": lax.rem(t + i, tp)},
            device_id_type=pl.DeviceIdType.MESH)

    def dq2_copy(i):
        return pltpu.make_async_remote_copy(
            src_ref=dqbuf.at[g], dst_ref=dqbuf.at[g], send_sem=dq2_send.at[i],
            recv_sem=dq2_recv.at[i], device_id={"group": lax.rem(g + i, groups)},
            device_id_type=pl.DeviceIdType.MESH)

    def dp_copy(i):
        dest = lax.rem(t + i, tp)
        return pltpu.make_async_remote_copy(
            src_ref=dpart.at[dest], dst_ref=dpeer.at[i], send_sem=dp_send.at[i],
            recv_sem=dp_recv.at[i], device_id={"tp": dest},
            device_id_type=pl.DeviceIdType.MESH)

    def da_copy(i):
        return pltpu.make_async_remote_copy(
            src_ref=dall.at[g], dst_ref=dall.at[g], send_sem=da_send.at[i],
            recv_sem=da_recv.at[i], device_id={"group": lax.rem(g + i, groups)},
            device_id_type=pl.DeviceIdType.MESH)

    q_copy = pltpu.make_async_copy(q_hbm, q_ref, loc_sem.at[0])
    dq0_copy = pltpu.make_async_copy(dq_hbm, dq_ref, loc_sem.at[1])
    ints = [pltpu.make_async_copy(src, dst, loc_sem.at[3 + i]) for i, (src, dst) in enumerate(
        ((off_hbm, off_ref), (own_hbm, own_ref), (len_hbm, len_ref)))]
    dkv_copy = pltpu.make_async_copy(dkv_hbm, dkv, loc_sem.at[2])
    dq0_copy.start()
    q_copy.start()
    for copy in ints:
        copy.start()
    for p in range(pieces):
        own_copy(p).start()

    barrier = pltpu.get_barrier_semaphore()
    for i in range(1, tp):
        pl.semaphore_signal(barrier, inc=1, device_id={"tp": lax.rem(t + i, tp)},
                            device_id_type=pl.DeviceIdType.MESH)
    for i in range(1, groups):
        pl.semaphore_signal(barrier, inc=1, device_id={"group": lax.rem(g + i, groups)},
                            device_id_type=pl.DeviceIdType.MESH)
    dq0_copy.wait()
    for r in range(served):
        for h in range(lh):
            dqtp[t, r, h:h + 1, :] = dq_ref[r:r + 1, h * HD:(h + 1) * HD].astype(jnp.float32)
    pl.semaphore_wait(barrier, tp - 1 + groups - 1)

    for i in range(1, tp):
        dq1_copy(i).start()
    early = [(2 * j + i, p) for j in range(1, chips) for p in range(pieces) for i in range(2)]
    cut = (chips - 1) * pieces // 2
    early, late = early[:2 * cut], early[2 * cut:]
    for s, p in early:
        kv_copy(s, p).start()
    for p in range(pieces):
        kv_copy(1, p).start()
    dkv_copy.start()
    acc[...] = jnp.zeros_like(acc)
    mrow[...] = jnp.full_like(mrow, LOW)
    for copy in ints:
        copy.wait()
    offset = off_ref[g]
    q_copy.wait()

    def split(b, carry):
        for e in range(stack):
            at = pl.ds(pl.multiple_of((b * stack + e) * HD, HD), HD)
            q = q_ref[:, at].astype(jnp.float32).T * SCALE
            high = q.astype(jnp.bfloat16)
            q2[b, :HD, e * rows:(e + 1) * rows] = high
            q2[b, HD:, e * rows:(e + 1) * rows] = (
                q - high.astype(jnp.float32)).astype(jnp.bfloat16)
        return carry

    lax.fori_loop(0, lh // stack, split, 0)
    vt[:, HD:, :] = jnp.ones((kvl, EXTRA, vt.shape[2]), jnp.bfloat16)

    def attend(parts, length):
        for e, (s, start) in enumerate(parts):
            at = pl.ds(e * length, length)
            pos = lax.broadcasted_iota(jnp.int32, (length, rows), 0) + (source(s) * llen + start)
            tok = lax.broadcasted_iota(jnp.int32, (length, rows), 1) + offset
            bias[at, :] = jnp.where(pos <= tok, 0.0, LOW)
            for k in range(kvl):
                vt[k, :HD, at] = kvbuf[s, 1, pl.ds(start, length), k * HD:(k + 1) * HD].T

        def some(b, carry):
            kv = b * stack // WIDTH
            kcol = pl.ds(pl.multiple_of(kv * HD, HD), HD)
            q = q2[b]
            old = mrow[b, :1, :]
            previous = acc[b]
            top = old
            scores = []
            for e, (s, start) in enumerate(parts):
                k = kvbuf[s, 0, pl.ds(start, length), kcol]
                sc = jnp.dot(jnp.concatenate([k, k], axis=1), q,
                             preferred_element_type=jnp.float32)
                mask = bias[pl.ds(e * length, length), :]
                sc = sc + jnp.concatenate([mask] * stack, axis=1)
                top = jnp.maximum(top, jnp.max(sc, axis=0, keepdims=True))
                scores.append(sc)
            out = previous * jnp.exp2(old - top)
            for e, sc in enumerate(scores):
                w = jnp.exp2(sc - top).astype(jnp.bfloat16)
                out += jnp.dot(vt[kv, :, pl.ds(e * length, length)], w,
                               preferred_element_type=jnp.float32)
            mrow[b] = jnp.broadcast_to(top, mrow.shape[1:])
            acc[b] = out
            return carry

        lax.fori_loop(0, lh // stack, some, 0)

    def far_step(b, carry):
        j, p = 1 + b // pieces, b % pieces
        for i in range(2):
            kv_copy(2 * j + i, p).wait_recv()
        start = pl.multiple_of(p * block, block)
        attend([(2 * j, start), (2 * j + 1, start)], block)
        return carry

    for p in range(pieces):
        own_copy(p).wait()
    attend([(0, p * block) for p in range(pieces)], block)

    for i in range(1, tp):
        dq1_copy(i).wait_recv()
    for r in range(served):
        whole = jnp.concatenate([dqtp[e, r] for e in range(tp)], axis=0)
        dqbuf[g, r] = whole.astype(jnp.bfloat16)
    for i in range(1, groups):
        dq2_copy(i).start()

    for p in range(pieces):
        kv_copy(1, p).wait_recv()
    attend([(1, p * block) for p in range(pieces)], block)

    dkv_copy.wait()
    for i in range(1, groups):
        dq2_copy(i).wait_recv()
    span = HD // slots
    lane = lax.broadcasted_iota(jnp.int32, (QH, HD), 1)
    stat = jnp.zeros((QH, HD), jnp.float32)
    for n in range(slots):
        owner = own_ref[g * slots + n]
        query = dqbuf[owner // served, owner % served].astype(jnp.float32)
        wide = jnp.concatenate([query.T] * KVH, axis=0)
        r = lax.broadcasted_iota(jnp.int32, (KVH * HD, QH), 0) // HD
        c = lax.broadcasted_iota(jnp.int32, (KVH * HD, QH), 1) // WIDTH
        wide = jnp.where(r == c, wide, 0.0).astype(jnp.bfloat16)
        sc = jnp.dot(dkv[n, 0], wide, preferred_element_type=jnp.float32).T
        pos = lax.broadcasted_iota(jnp.int32, (QH, slen), 1) + t * slen
        live = pos < len_ref[g * slots + n]
        sc = jnp.where(live, sc * SCALE, LOW)
        top = jnp.max(sc, axis=1, keepdims=True)
        w = jnp.where(live, jnp.exp2(sc - top), 0.0).astype(jnp.bfloat16)
        total = jnp.sum(w.astype(jnp.float32), axis=1, keepdims=True)
        o = jnp.dot(w, dkv[n, 1], preferred_element_type=jnp.float32)
        o = jnp.concatenate(
            [o[k * WIDTH:(k + 1) * WIDTH, k * HD:(k + 1) * HD] for k in range(KVH)], axis=0)
        stat = jnp.where(lane == n * span, top, stat)
        stat = jnp.where(lane == n * span + 1, total, stat)
        for d in range(tp):
            dpart[d, n] = o[d * lh:(d + 1) * lh]
    for d in range(tp):
        dpart[d, slots] = stat[d * lh:(d + 1) * lh]
    for i in range(1, tp):
        dp_copy(i).start()
    for s, p in late:
        kv_copy(s, p).start()

    far = (chips - 1) * pieces
    lax.fori_loop(0, cut, far_step, 0)

    for i in range(1, tp):
        dp_copy(i).wait_recv()
    lane = lax.broadcasted_iota(jnp.int32, (lh, HD), 1)
    joined = jnp.zeros((lh, HD), jnp.float32)
    stats = [dpart[t, slots]] + [dpeer[i, slots] for i in range(1, tp)]
    for n in range(slots):
        accs = [dpart[t, n]] + [dpeer[i, n] for i in range(1, tp)]
        at = n * span
        top = functools.reduce(jnp.maximum, [x[:, at:at + 1] for x in stats])
        fac = [jnp.exp2(x[:, at:at + 1] - top) for x in stats]
        total = sum(f * x[:, at + 1:at + 2] for f, x in zip(fac, stats))
        dall[g, n] = sum(f * a for f, a in zip(fac, accs))
        joined = jnp.where(lane == at, top, joined)
        joined = jnp.where(lane == at + 1, total, joined)
    dall[g, slots] = joined
    for i in range(1, groups):
        da_copy(i).start()

    lax.fori_loop(cut, far, far_step, 0)

    def finish(b, carry):
        a = acc[b]
        a = a[:HD] / a[HD:HD + 1]
        for e in range(stack):
            at = pl.ds(pl.multiple_of((b * stack + e) * HD, HD), HD)
            out_ref[:, at] = a[:, e * rows:(e + 1) * rows].T.astype(out_ref.dtype)
        return carry

    lax.fori_loop(0, lh // stack, finish, 0)

    for i in range(1, groups):
        da_copy(i).wait_recv()
    for r in range(served):
        mine = g * served + r

        def peak(e, top):
            for n in range(slots):
                m = jnp.broadcast_to(dall[e, slots][:, n * span:n * span + 1], (lh, HD))
                top = jnp.maximum(top, jnp.where(own_ref[e * slots + n] == mine, m, LOW))
            return top

        top = lax.fori_loop(0, groups, peak, jnp.full((lh, HD), LOW, jnp.float32))

        def gather(e, carry):
            num, den = carry
            for n in range(slots):
                x = dall[e, slots][:, n * span:n * span + 2]
                hit = own_ref[e * slots + n] == mine
                f = jnp.where(hit, jnp.exp2(jnp.minimum(x[:, :1] - top, 0.0)), 0.0)
                num = num + f * dall[e, n]
                den = den + f * x[:, 1:2]
            return num, den

        zero = jnp.zeros((lh, HD), jnp.float32)
        num, den = lax.fori_loop(0, groups, gather, (zero, zero))
        res = num / den
        for h in range(lh):
            dout_ref[r:r + 1, h * HD:(h + 1) * HD] = res[h:h + 1].astype(dout_ref.dtype)

    for i in range(1, tp):
        dq1_copy(i).wait_send()
        dp_copy(i).wait_send()
    for i in range(1, groups):
        dq2_copy(i).wait_send()
        da_copy(i).wait_send()
    for s in range(1, tp):
        for p in range(pieces):
            kv_copy(s, p).wait_send()


def on_device(pf_query, pf_cache, pf_offset, dec_query, dec_cache, slot_owner, slot_len):
    tp = lax.axis_size("tp")
    groups = lax.axis_size("group")
    rows, llen = pf_query.shape[0], pf_cache.shape[2]
    lh = QH // tp
    kvl = max(1, lh // WIDTH)
    served, slots, slen = dec_query.shape[0], dec_cache.shape[0], dec_cache.shape[2]
    block = min(512, llen)
    pieces = llen // block
    span = max(2 * block, llen)
    cfg = (tp, groups, rows, llen, block, STACK, lh, kvl, served, slots, slen)
    dma = pltpu.SemaphoreType.DMA
    anywhere = pl.BlockSpec(memory_space=pl.ANY)
    vmem = pl.BlockSpec(memory_space=pltpu.VMEM)
    pf_out, dec_out = pl.pallas_call(
        functools.partial(kernel, cfg),
        out_shape=(
            jax.ShapeDtypeStruct((rows, lh * HD), jnp.bfloat16),
            jax.ShapeDtypeStruct((served, lh * HD), jnp.bfloat16),
        ),
        in_specs=[anywhere] * 7,
        out_specs=(vmem, vmem),
        scratch_shapes=[
            pltpu.SMEM(pf_offset.shape, jnp.int32),
            pltpu.SMEM(slot_owner.shape, jnp.int32),
            pltpu.SMEM(slot_len.shape, jnp.int32),
            pltpu.VMEM((rows, lh * HD), jnp.bfloat16),
            pltpu.VMEM((served, lh * HD), jnp.bfloat16),
            pltpu.VMEM((lh // STACK, 2 * HD, STACK * rows), jnp.bfloat16),
            pltpu.VMEM((tp, 2, llen, kvl * HD), jnp.bfloat16),
            pltpu.VMEM(dec_cache.shape, jnp.bfloat16),
            pltpu.VMEM((kvl, HD + EXTRA, span), jnp.bfloat16),
            pltpu.VMEM((span, rows), jnp.float32),
            pltpu.VMEM((lh // STACK, HD + EXTRA, STACK * rows), jnp.float32),
            pltpu.VMEM((lh // STACK, 8, STACK * rows), jnp.float32),
            pltpu.VMEM((tp, served, lh, HD), jnp.float32),
            pltpu.VMEM((groups, served, QH, HD), jnp.bfloat16),
            pltpu.VMEM((tp, slots + 1, lh, HD), jnp.float32),
            pltpu.VMEM((tp, slots + 1, lh, HD), jnp.float32),
            pltpu.VMEM((groups, slots + 1, lh, HD), jnp.float32),
            dma((6,)),
            dma((pieces,)),
            dma((tp, pieces)),
            dma((tp, pieces)),
            dma((tp,)),
            dma((tp,)),
            dma((groups,)),
            dma((groups,)),
            dma((tp,)),
            dma((tp,)),
            dma((groups,)),
            dma((groups,)),
        ],
        compiler_params=pltpu.CompilerParams(
            collective_id=0, has_side_effects=True, vmem_limit_bytes=60 * 1024 * 1024),
    )(pf_offset, slot_owner, slot_len, pf_query, pf_cache, dec_query, dec_cache)
    return pf_out, dec_out


def solution(mesh):
    placed = (
        P("group", "tp"),
        P("group", None, "tp", None),
        P(),
        P("group", "tp"),
        P("group", None, "tp", None),
        P(),
        P(),
    )
    return jax.shard_map(
        on_device,
        mesh=mesh,
        in_specs=placed,
        out_specs=(P("group", "tp"), P("group", "tp")),
        check_vma=False,
    )
```

time: 81.1 us -> 72.2 us (0.89)
  Pallas kernels: 74.8 us -> 67.1 us
  local copies, waits for them, and re-layouts: 4.76 us -> 3.61 us
    pallas_call x1, Pallas kernels: 74.8 us -> 67.1 us  [on_device(): pl.pallas_call(functools.partial(kernel, cfg), out_shape=(jax.ShapeDtypeS...]
    unnamed x11 -> x2, local copies, waits for them, and re-layouts: 4.76 us -> 3.61 us
where the time goes in v2:
time: 72.2 us; the launch traced here: 71.4 us
  Pallas kernels  67.1 us (93%)
  local copies, waits for them, and re-layouts  3.61 us (5%)
    pallas_call x1, Pallas kernels, on_device(): pl.pallas_call(functools.partial(kernel, cfg), out_shape=(jax.ShapeDtypeS...  67.1 us
    unnamed x2, local copies, waits for them, and re-layouts  3.61 us

profile of v2, /device:TPU:0, one launch (start us, length us, event | category | flops | bytes accessed | tf_op | source)
XLA Modules:
  0.0 71.4 jit_solution(1245309424278130411)
XLA Ops:
  0.6 67.1 %shard_map.86 = (bf16[256,2048]{1,0:T(8,128)(2,1)}, bf16[2,2048]{1,0:T(2,128)(2,1)}) custom-call(s32[8]{0:T(128)} %off_hbm.1, s32[24]{0:T(128)} %own_hbm.1, s32[24]{0:T(128)} %len_hbm.1, bf16[256,2048]{1,0:T(8,128)(2,1)} %q_hbm.1, bf16[1,2,1024,1024]{3,2,1,0:T(8,128)(2,1)} %kv_hbm.1, bf16[2,2048]{1,0:T(2,128)(2,1)} %dq_hbm.1, bf16[3,2,512,1024]{3,2,1,0:T(8,128)(2,1)} %dkv_hbm.1), custom_call_target="tpu_custom_call" | custom-call | tf_op jit(solution)/shard_map/pallas_call | solution.py:318
  67.8 2.3 %copy.11 = bf16[256,2048]{1,0:T(8,128)(2,1)} copy(bf16[256,2048]{1,0:T(8,128)(2,1)} %get-tuple-element.4) | data formatting | bytes 2097152
  70.1 1.3 %copy.12 = bf16[2,2048]{1,0:T(2,128)(2,1)} copy(bf16[2,2048]{1,0:T(2,128)(2,1)} %get-tuple-element.5) | data formatting | bytes 16384

commit v3 on v2

--- a/solution.py
+++ b/solution.py
@@ -12,7 +12,7 @@
 HD = 128
 WIDTH = QH // KVH
 LOW = -1e30
-STACK = 2
+STACK = 4
 EXTRA = 16
 SCALE = HD ** (-0.5) * math.log2(math.e)
 
@@ -308,7 +308,7 @@
     lh = QH // tp
     kvl = max(1, lh // WIDTH)
     served, slots, slen = dec_query.shape[0], dec_cache.shape[0], dec_cache.shape[2]
-    block = min(512, llen)
+    block = min(256, llen)
     pieces = llen // block
     span = max(2 * block, llen)
     cfg = (tp, groups, rows, llen, block, STACK, lh, kvl, served, slots, slen)

time: 72.2 us -> 68.1 us (0.943)
  Pallas kernels: 67.1 us -> 63.1 us
    pallas_call x1, Pallas kernels: 67.1 us -> 63.1 us  [on_device(): pl.pallas_call(functools.partial(kernel, cfg), out_shape=(jax.ShapeDtypeS...]
where the time goes in v3:
time: 68.1 us; the launch traced here: 67.3 us
  Pallas kernels  63.1 us (93%)
  local copies, waits for them, and re-layouts  3.61 us (5%)
    pallas_call x1, Pallas kernels, on_device(): pl.pallas_call(functools.partial(kernel, cfg), out_shape=(jax.ShapeDtypeS...  63.1 us
    unnamed x2, local copies, waits for them, and re-layouts  3.61 us

profile of v3, /device:TPU:0, one launch (start us, length us, event | category | flops | bytes accessed | tf_op | source)
XLA Modules:
  0.0 67.3 jit_solution(346496730719723583)
XLA Ops:
  0.6 63.1 %shard_map.86 = (bf16[256,2048]{1,0:T(8,128)(2,1)}, bf16[2,2048]{1,0:T(2,128)(2,1)}) custom-call(s32[8]{0:T(128)} %off_hbm.1, s32[24]{0:T(128)} %own_hbm.1, s32[24]{0:T(128)} %len_hbm.1, bf16[256,2048]{1,0:T(8,128)(2,1)} %q_hbm.1, bf16[1,2,1024,1024]{3,2,1,0:T(8,128)(2,1)} %kv_hbm.1, bf16[2,2048]{1,0:T(2,128)(2,1)} %dq_hbm.1, bf16[3,2,512,1024]{3,2,1,0:T(8,128)(2,1)} %dkv_hbm.1), custom_call_target="tpu_custom_call" | custom-call | tf_op jit(solution)/shard_map/pallas_call | solution.py:318
  63.7 2.3 %copy.11 = bf16[256,2048]{1,0:T(8,128)(2,1)} copy(bf16[256,2048]{1,0:T(8,128)(2,1)} %get-tuple-element.4) | data formatting | bytes 2097152
  66.0 1.3 %copy.12 = bf16[2,2048]{1,0:T(2,128)(2,1)} copy(bf16[2,2048]{1,0:T(2,128)(2,1)} %get-tuple-element.5) | data formatting | bytes 16384
